TPU v7x, 1024 devices: a whole 8x8x8 slice. The times are simulated.
1024 devices in a mesh: front: 16 (over z, core), row: 8 (over y), col: 8 (over x).
Axes of the slice: x: 8, y: 8, z: 8, core: 2. Of those that a mesh axis runs over, the one named last changes fastest.
Arguments:
- tile: float32 [16, 2048, 4096], P('front', 'row', 'col'), may hold values from -6 to 6
- top_block: float32 [16, 256, 4096], P('front', None, 'col'), may hold values from -6 to 6
- reflectors: float32 [16, 2048, 256], P('front', 'row'), may hold values from -0.375 to 0.375
- panel_t: float32 [16, 2048, 256], P('front', 'row'), as said below
- parent: int32 [16], replicated, may hold values from 0 to 65535
- send_rows: int32 [16, 8, 8, 32], P('front', 'row'), may hold values from 0 to 255, as said below
- send_count: int32 [16, 8, 8], P('front', 'row'), may hold values from 24 to 32, as said below
- parent_reflectors: float32 [16, 4096, 256], P('front', 'row'), may hold values from -0.25 to 0.25
- parent_t: float32 [16, 2048, 256], P('front', 'row'), as said below
Outputs:
- renewed_tile: float32 [16, 2048, 4096], P('front', 'row', 'col')
- top_after: float32 [16, 2048, 4096], P('front', 'row', 'col')
- assembled: float32 [16, 4096, 4096], P('front', 'row', 'col')
Inputs may be any that keep to these rules, and one draw needn't show every extreme that they name: `send_rows`: within one row owner of one front the listed indices are distinct rows of its 256 rows. `send_count`: each row owner of each front has a slot that sends exactly 32 rows. `panel_t`: upper triangular. `parent_t`: upper triangular.
All inputs are finite; a program needn't handle non-finite values.
Results may differ from a plain program's by a relative error of at most 0.0003.
Values sent between devices are 32-bit elements; how exact they have to be, the bound alone decides.
A program may use at most 64 MiB of HBM per device.

v0:
```python
import jax
import jax.numpy as jnp
from jax import lax
from jax.sharding import PartitionSpec as P

PRECISION = lax.Precision.HIGHEST


def passed_along(shard, axis, by):
    length = lax.axis_size(axis)
    pairs = [(i, i + by) for i in range(length) if 0 <= i + by < length]
    return lax.ppermute(shard, axis, pairs)


def product(left, right):
    return jnp.dot(left, right, precision=PRECISION, preferred_element_type=jnp.float32)


def transposed(left, right):
    return lax.dot_general(
        left,
        right,
        (((0,), (0,)), ((), ())),
        precision=PRECISION,
        preferred_element_type=jnp.float32,
    )


def shards(
    tile, top_block, reflectors, panel_t, parent, send_rows, send_count, parent_reflectors, parent_t
):
    own_tile = tile[0]
    vectors = reflectors[0]
    factor = panel_t[0]
    initial = top_block[0]
    projected = transposed(vectors, own_tile)
    position = lax.axis_index("row")

    def advance(number, entering):
        leaving = entering - transposed(factor, entering + projected)
        arrived = passed_along(leaving, "row", 1)
        return jnp.where(position == 0, initial, arrived)

    entering = lax.fori_loop(0, lax.axis_size("row") - 1, advance, initial)
    update = transposed(factor, entering + projected)
    leaving = entering - update
    renewed = own_tile - product(vectors, update)
    indices = send_rows[0, 0]
    counts = send_count[0, 0]
    spread = indices.shape[0]
    capacity = indices.shape[1]
    chosen = renewed[indices.reshape(-1)].reshape(spread, capacity, renewed.shape[1])
    occupied = (jnp.arange(capacity, dtype=jnp.int32)[None, :] < counts[:, None]).astype(
        jnp.float32
    )
    chosen = chosen * occupied[:, :, None]
    groups = lax.axis_size("front")
    parent_group = parent[lax.axis_index("front")]
    offsets = jnp.mod(jnp.arange(groups, dtype=jnp.int32) - parent_group, groups)
    usable = (offsets < spread).astype(jnp.float32)
    outgoing = chosen[jnp.minimum(offsets, spread - 1)] * usable[:, None, None]
    parent_vectors = parent_reflectors[0]
    parent_factor = parent_t[0]
    received = lax.all_to_all(outgoing, "front", split_axis=0, concat_axis=0, tiled=True)
    stacked = received.reshape(-1, received.shape[2])
    inner_sums = transposed(parent_vectors, stacked)
    weights = transposed(parent_factor, inner_sums)
    assembled = stacked - product(parent_vectors, weights)
    return (renewed[None], leaving[None], assembled[None])


def solution(mesh):
    placed = (
        P("front", "row", "col"),
        P("front", None, "col"),
        P("front", "row", None),
        P("front", "row", None),
        P(),
        P("front", "row", None, None),
        P("front", "row", None),
        P("front", "row", None),
        P("front", "row", None),
    )
    return jax.shard_map(
        shards,
        mesh=mesh,
        in_specs=placed,
        out_specs=(P("front", "row", "col"), P("front", "row", "col"), P("front", "row", "col")),
        check_vma=False,
    )
```

profile of v0, /device:TPU:77, one launch (start us, length us, event | category | flops | bytes accessed | tf_op | source)
XLA Modules:
  0.0 172.7 jit_solution(16218025008148021154)
XLA Ops:
  0.7 0.7 copy-done.14
  4.8 2.1 %copy.20 = f32[1,256,512]{1,2,0:T(8,128)} copy(f32[1,256,512]{2,1,0:T(8,128)} %param.11) | data formatting | bytes 1048576 | tf_op args[0]
  7.6 0.8 copy-done.2
  8.5 0.8 copy-done.10
  9.6 0.9 copy-done.1
  10.5 97.2 %while.12 = (s32[]{:T(128)}, f32[256,512]{0,1:T(8,128)S(1)}, pred[]{:T(512)}, f32[256,512]{0,1:T(8,128)S(1)}, f32[256,256]{1,0:T(8,128)S(1)}, /*index=5*/f32[256,512]{0,1:T(8,128)S(1)}, s32[]{:T(128)}) while((s32[]{:T(128)}, f32[256,512]{0,1:T(8,128)S(1)}, pred[]{:T(512)}, f32[256,512]{0,1:T(8,128)S(1)}, f32[256,256]{1,0:T(8,128)S(1)}, ...), condition=%wide.region_1.2_spmd, body=%wide.region_0.1_spmd.sunk | while | flops 403046400 | bytes 5505142 | solution.py:44
  11.1 2.4 %collective-permute-start = (f32[256,512]{0,1:T(8,128)S(1)}, f32[256,512]{0,1:T(8,128)S(1)}, u32[]{:S(2)}, u32[]{:S(2)}) collective-permute-start(f32[256,512]{0,1:T(8,128)S(1)} %fusion.33), channel_id=1, source_target_pairs={{0,8},{8,16},{16,24},{24,32},{32,40},{40,48},{48,56},{1,9},{9,17},... | collective-permute-start | bytes 1572872 | tf_op jit(solution)/shard_map/while/body/eval_jaxpr/ppermute | solution.py:12
  13.6 13.5 %collective-permute-done = f32[256,512]{0,1:T(8,128)S(1)} collective-permute-done((f32[256,512]{0,1:T(8,128)S(1)}, f32[256,512]{0,1:T(8,128)S(1)}, u32[]{:S(2)}, u32[]{:S(2)}) %collective-permute-start) | collective-permute-done | bytes 524320 | tf_op jit(solution)/shard_map/while/body/eval_jaxpr/ppermute | solution.py:12
  27.7 1.9 %collective-permute-start = (f32[256,512]{0,1:T(8,128)S(1)}, f32[256,512]{0,1:T(8,128)S(1)}, u32[]{:S(2)}, u32[]{:S(2)}) collective-permute-start(f32[256,512]{0,1:T(8,128)S(1)} %fusion.33), channel_id=1, source_target_pairs={{0,8},{8,16},{16,24},{24,32},{32,40},{40,48},{48,56},{1,9},{9,17},... | collective-permute-start | bytes 1572872 | tf_op jit(solution)/shard_map/while/body/eval_jaxpr/ppermute | solution.py:12
  29.6 13.0 %collective-permute-done = f32[256,512]{0,1:T(8,128)S(1)} collective-permute-done((f32[256,512]{0,1:T(8,128)S(1)}, f32[256,512]{0,1:T(8,128)S(1)}, u32[]{:S(2)}, u32[]{:S(2)}) %collective-permute-start) | collective-permute-done | bytes 524320 | tf_op jit(solution)/shard_map/while/body/eval_jaxpr/ppermute | solution.py:12
  43.4 1.9 %collective-permute-start = (f32[256,512]{0,1:T(8,128)S(1)}, f32[256,512]{0,1:T(8,128)S(1)}, u32[]{:S(2)}, u32[]{:S(2)}) collective-permute-start(f32[256,512]{0,1:T(8,128)S(1)} %fusion.33), channel_id=1, source_target_pairs={{0,8},{8,16},{16,24},{24,32},{32,40},{40,48},{48,56},{1,9},{9,17},... | collective-permute-start | bytes 1572872 | tf_op jit(solution)/shard_map/while/body/eval_jaxpr/ppermute | solution.py:12
  45.3 12.1 %collective-permute-done = f32[256,512]{0,1:T(8,128)S(1)} collective-permute-done((f32[256,512]{0,1:T(8,128)S(1)}, f32[256,512]{0,1:T(8,128)S(1)}, u32[]{:S(2)}, u32[]{:S(2)}) %collective-permute-start) | collective-permute-done | bytes 524320 | tf_op jit(solution)/shard_map/while/body/eval_jaxpr/ppermute | solution.py:12
  58.1 1.9 %collective-permute-start = (f32[256,512]{0,1:T(8,128)S(1)}, f32[256,512]{0,1:T(8,128)S(1)}, u32[]{:S(2)}, u32[]{:S(2)}) collective-permute-start(f32[256,512]{0,1:T(8,128)S(1)} %fusion.33), channel_id=1, source_target_pairs={{0,8},{8,16},{16,24},{24,32},{32,40},{40,48},{48,56},{1,9},{9,17},... | collective-permute-start | bytes 1572872 | tf_op jit(solution)/shard_map/while/body/eval_jaxpr/ppermute | solution.py:12
  60.0 11.2 %collective-permute-done = f32[256,512]{0,1:T(8,128)S(1)} collective-permute-done((f32[256,512]{0,1:T(8,128)S(1)}, f32[256,512]{0,1:T(8,128)S(1)}, u32[]{:S(2)}, u32[]{:S(2)}) %collective-permute-start) | collective-permute-done | bytes 524320 | tf_op jit(solution)/shard_map/while/body/eval_jaxpr/ppermute | solution.py:12
  71.9 1.9 %collective-permute-start = (f32[256,512]{0,1:T(8,128)S(1)}, f32[256,512]{0,1:T(8,128)S(1)}, u32[]{:S(2)}, u32[]{:S(2)}) collective-permute-start(f32[256,512]{0,1:T(8,128)S(1)} %fusion.33), channel_id=1, source_target_pairs={{0,8},{8,16},{16,24},{24,32},{32,40},{40,48},{48,56},{1,9},{9,17},... | collective-permute-start | bytes 1572872 | tf_op jit(solution)/shard_map/while/body/eval_jaxpr/ppermute | solution.py:12
  73.8 10.3 %collective-permute-done = f32[256,512]{0,1:T(8,128)S(1)} collective-permute-done((f32[256,512]{0,1:T(8,128)S(1)}, f32[256,512]{0,1:T(8,128)S(1)}, u32[]{:S(2)}, u32[]{:S(2)}) %collective-permute-start) | collective-permute-done | bytes 524320 | tf_op jit(solution)/shard_map/while/body/eval_jaxpr/ppermute | solution.py:12
  84.8 1.9 %collective-permute-start = (f32[256,512]{0,1:T(8,128)S(1)}, f32[256,512]{0,1:T(8,128)S(1)}, u32[]{:S(2)}, u32[]{:S(2)}) collective-permute-start(f32[256,512]{0,1:T(8,128)S(1)} %fusion.33), channel_id=1, source_target_pairs={{0,8},{8,16},{16,24},{24,32},{32,40},{40,48},{48,56},{1,9},{9,17},... | collective-permute-start | bytes 1572872 | tf_op jit(solution)/shard_map/while/body/eval_jaxpr/ppermute | solution.py:12
  86.7 9.2 %collective-permute-done = f32[256,512]{0,1:T(8,128)S(1)} collective-permute-done((f32[256,512]{0,1:T(8,128)S(1)}, f32[256,512]{0,1:T(8,128)S(1)}, u32[]{:S(2)}, u32[]{:S(2)}) %collective-permute-start) | collective-permute-done | bytes 524320 | tf_op jit(solution)/shard_map/while/body/eval_jaxpr/ppermute | solution.py:12
  96.6 1.9 %collective-permute-start = (f32[256,512]{0,1:T(8,128)S(1)}, f32[256,512]{0,1:T(8,128)S(1)}, u32[]{:S(2)}, u32[]{:S(2)}) collective-permute-start(f32[256,512]{0,1:T(8,128)S(1)} %fusion.33), channel_id=1, source_target_pairs={{0,8},{8,16},{16,24},{24,32},{32,40},{40,48},{48,56},{1,9},{9,17},... | collective-permute-start | bytes 1572872 | tf_op jit(solution)/shard_map/while/body/eval_jaxpr/ppermute | solution.py:12
  98.5 9.2 %collective-permute-done = f32[256,512]{0,1:T(8,128)S(1)} collective-permute-done((f32[256,512]{0,1:T(8,128)S(1)}, f32[256,512]{0,1:T(8,128)S(1)}, u32[]{:S(2)}, u32[]{:S(2)}) %collective-permute-start) | collective-permute-done | bytes 524320 | tf_op jit(solution)/shard_map/while/body/eval_jaxpr/ppermute | solution.py:12
  108.0 0.8 copy-done.3
  108.8 1.0 fusion.11
  110.8 1.8 %gather_fusion = f32[256,512]{1,0:T(8,128)} fusion(f32[256,512]{1,0:T(8,128)S(1)} %copy.24, s32[1024]{0:T(1024)S(1)} %pad_clamp_fusion.1), kind=kCustom, calls=%fused_computation | custom fusion | bytes 1049600 | tf_op jit(solution)/shard_map/gather | solution.py:52
  112.5 1.1 broadcast_multiply_fusion.1
  114.3 1.1 broadcast_multiply_fusion
  115.4 24.2 %all-to-all-start = ((f32[16,32,512]{2,1,0:T(8,128)}), f32[16,32,512]{2,1,0:T(8,128)S(1)}, u32[]{:S(2)}, u32[]{:S(2)}) async-start(f32[16,32,512]{2,1,0:T(8,128)} %broadcast_multiply_fusion), calls=%async_computation | async-start | bytes 2097152 | tf_op jit(solution)/shard_map/all_to_all | solution.py:64
  139.7 1.0 copy.27
  140.7 1.0 copy.26
  141.7 25.8 %all-to-all-done = f32[16,32,512]{2,1,0:T(8,128)S(1)} async-done(((f32[16,32,512]{2,1,0:T(8,128)}), f32[16,32,512]{2,1,0:T(8,128)S(1)}, u32[]{:S(2)}, u32[]{:S(2)}) %all-to-all-start) | async-done | bytes 1048608 | tf_op jit(solution)/shard_map/all_to_all | solution.py:64
  167.9 1.8 %fusion.8 = f32[512,256]{1,0:T(8,128)S(1)} fusion(f32[512,512]{1,0:T(8,128)S(1)} %bitcast.68, f32[1,512,256]{2,1,0:T(8,128)S(1)} %copy-done), kind=kOutput, calls=%fused_computation.14 | convolution fusion | flops 805306368 | bytes 2097152 | tf_op jit(solution)/shard_map/dot_general | solution.py:20
  170.3 1.0 fusion.3
  171.4 1.3 copy.28
  (58 shorter events, 11.8 us)
Async XLA Ops:
  0.6 167.3 %copy-start = (f32[1,512,256]{2,1,0:T(8,128)S(1)}, f32[1,512,256]{2,1,0:T(8,128)}, u32[]{:S(2)}) copy-start(f32[1,512,256]{2,1,0:T(8,128)} %param.18) | copy-start | bytes 1572868
  0.7 0.7 copy-start.14
  3.3 0.7 copy-start.12
  4.1 0.7 copy-start.13
  4.8 2.1 %copy-start.7 = (f32[1,256,512]{2,1,0:T(8,128)S(1)}, f32[1,256,512]{2,1,0:T(8,128)}, u32[]{:S(2)}) copy-start(f32[1,256,512]{2,1,0:T(8,128)} %param.11) | copy-start | bytes 1572868
  4.8 2.1 %copy-start.8 = (f32[1,256,256]{2,1,0:T(8,128)S(1)}, f32[1,256,256]{2,1,0:T(8,128)}, u32[]{:S(2)}) copy-start(f32[1,256,256]{2,1,0:T(8,128)} %param.13) | copy-start | bytes 786436
  7.5 0.8 copy-start.2
  8.3 1.0 copy-start.10
  9.6 1.0 copy-start.1
  11.1 15.9 %collective-permute-start = (f32[256,512]{0,1:T(8,128)S(1)}, f32[256,512]{0,1:T(8,128)S(1)}, u32[]{:S(2)}, u32[]{:S(2)}) collective-permute-start(f32[256,512]{0,1:T(8,128)S(1)} %fusion.33), channel_id=1, source_target_pairs={{0,8},{8,16},{16,24},{24,32},{32,40},{40,48},{48,56},{1,9},{9,17},... | collective-permute-start | bytes 1572872 | tf_op jit(solution)/shard_map/while/body/eval_jaxpr/ppermute | solution.py:12
  27.7 15.0 %collective-permute-start = (f32[256,512]{0,1:T(8,128)S(1)}, f32[256,512]{0,1:T(8,128)S(1)}, u32[]{:S(2)}, u32[]{:S(2)}) collective-permute-start(f32[256,512]{0,1:T(8,128)S(1)} %fusion.33), channel_id=1, source_target_pairs={{0,8},{8,16},{16,24},{24,32},{32,40},{40,48},{48,56},{1,9},{9,17},... | collective-permute-start | bytes 1572872 | tf_op jit(solution)/shard_map/while/body/eval_jaxpr/ppermute | solution.py:12
  43.4 14.0 %collective-permute-start = (f32[256,512]{0,1:T(8,128)S(1)}, f32[256,512]{0,1:T(8,128)S(1)}, u32[]{:S(2)}, u32[]{:S(2)}) collective-permute-start(f32[256,512]{0,1:T(8,128)S(1)} %fusion.33), channel_id=1, source_target_pairs={{0,8},{8,16},{16,24},{24,32},{32,40},{40,48},{48,56},{1,9},{9,17},... | collective-permute-start | bytes 1572872 | tf_op jit(solution)/shard_map/while/body/eval_jaxpr/ppermute | solution.py:12
  58.1 13.1 %collective-permute-start = (f32[256,512]{0,1:T(8,128)S(1)}, f32[256,512]{0,1:T(8,128)S(1)}, u32[]{:S(2)}, u32[]{:S(2)}) collective-permute-start(f32[256,512]{0,1:T(8,128)S(1)} %fusion.33), channel_id=1, source_target_pairs={{0,8},{8,16},{16,24},{24,32},{32,40},{40,48},{48,56},{1,9},{9,17},... | collective-permute-start | bytes 1572872 | tf_op jit(solution)/shard_map/while/body/eval_jaxpr/ppermute | solution.py:12
  71.9 12.2 %collective-permute-start = (f32[256,512]{0,1:T(8,128)S(1)}, f32[256,512]{0,1:T(8,128)S(1)}, u32[]{:S(2)}, u32[]{:S(2)}) collective-permute-start(f32[256,512]{0,1:T(8,128)S(1)} %fusion.33), channel_id=1, source_target_pairs={{0,8},{8,16},{16,24},{24,32},{32,40},{40,48},{48,56},{1,9},{9,17},... | collective-permute-start | bytes 1572872 | tf_op jit(solution)/shard_map/while/body/eval_jaxpr/ppermute | solution.py:12
  84.8 11.1 %collective-permute-start = (f32[256,512]{0,1:T(8,128)S(1)}, f32[256,512]{0,1:T(8,128)S(1)}, u32[]{:S(2)}, u32[]{:S(2)}) collective-permute-start(f32[256,512]{0,1:T(8,128)S(1)} %fusion.33), channel_id=1, source_target_pairs={{0,8},{8,16},{16,24},{24,32},{32,40},{40,48},{48,56},{1,9},{9,17},... | collective-permute-start | bytes 1572872 | tf_op jit(solution)/shard_map/while/body/eval_jaxpr/ppermute | solution.py:12
  96.6 11.1 %collective-permute-start = (f32[256,512]{0,1:T(8,128)S(1)}, f32[256,512]{0,1:T(8,128)S(1)}, u32[]{:S(2)}, u32[]{:S(2)}) collective-permute-start(f32[256,512]{0,1:T(8,128)S(1)} %fusion.33), channel_id=1, source_target_pairs={{0,8},{8,16},{16,24},{24,32},{32,40},{40,48},{48,56},{1,9},{9,17},... | collective-permute-start | bytes 1572872 | tf_op jit(solution)/shard_map/while/body/eval_jaxpr/ppermute | solution.py:12
  107.8 1.0 copy-start.3
  108.8 1.0 copy-start.6
  108.8 1.1 copy-start.9
  110.6 2.0 %copy-start.4 = (f32[256,512]{0,1:T(8,128)}, f32[256,512]{0,1:T(8,128)S(1)}, u32[]{:S(2)}) copy-start(f32[256,512]{0,1:T(8,128)S(1)} %fusion.4) | copy-start | bytes 1572868
  115.4 52.1 %all-to-all-start = ((f32[16,32,512]{2,1,0:T(8,128)}), f32[16,32,512]{2,1,0:T(8,128)S(1)}, u32[]{:S(2)}, u32[]{:S(2)}) async-start(f32[16,32,512]{2,1,0:T(8,128)} %broadcast_multiply_fusion), calls=%async_computation | async-start | bytes 2097152 | tf_op jit(solution)/shard_map/all_to_all | solution.py:64
  139.7 1.0 copy-start.5
  167.9 1.8 %copy-start.11 = (f32[1,256,256]{2,1,0:T(8,128)S(1)}, f32[1,256,256]{2,1,0:T(8,128)}, u32[]{:S(2)}) copy-start(f32[1,256,256]{2,1,0:T(8,128)} %param.19) | copy-start | bytes 786436
where the time goes:
time: 173 us
  waiting for transfers between devices  104 us (60%)
  starting transfers between devices  38.1 us (22%)
  local copies, waits for them, and re-layouts  15.1 us (9%)
  matrix products  9.77 us (6%)
  other arithmetic  4.19 us (2%)
    ppermute x7, waiting for transfers between devices, passed_along(): return lax.ppermute(shard, axis, pairs)  78.5 us
    all_to_all x1, waiting for transfers between devices, shards(): lax.all_to_all(outgoing, 'front', split_axis=0, concat_axis=0, tiled=True)  25.8 us
    all_to_all x1, starting transfers between devices, shards(): lax.all_to_all(outgoing, 'front', split_axis=0, concat_axis=0, tiled=True)  24.2 us
    ppermute x7, starting transfers between devices, passed_along(): return lax.ppermute(shard, axis, pairs)  13.9 us
    unnamed x36, local copies, waits for them, and re-layouts  11.2 us
    dot_general x11, matrix products, transposed(): lax.dot_general(left, right, (((0,), (0,)), ((), ())), precision=PRECISIO...  8.11 us
  transfers between devices with their start and end apart: 8, of which 8 were waited for; matrix products, arithmetic and copies ran while one was open for 1% of the time, Pallas kernels for 0%

commit v1 on v0

v1 whole, which is shorter than its diff:
```python
import functools

import jax
import jax.numpy as jnp
from jax import lax
from jax.experimental import pallas as pl
from jax.experimental.pallas import tpu as pltpu
from jax.sharding import PartitionSpec as P

MESH = pl.DeviceIdType.MESH
F32, BF16 = jnp.float32, jnp.bfloat16
CHUNK = 128
PIECES = 4


def split(x):
    high = x.astype(BF16)
    return high, (x - high.astype(F32)).astype(BF16)


def dot(left, right):
    return jnp.dot(left, right, preferred_element_type=F32)


def left_triple(x):
    high, low = split(x)
    return jnp.concatenate([high, high, low], axis=1)


def right_triple(x):
    high, low = split(x)
    return jnp.concatenate([high, low, high], axis=0)


def kernel(
    n_front,
    n_row,
    tile_in,
    top_in,
    vectors_in,
    factor_in,
    rows_in,
    pvectors_in,
    pfactor_in,
    parent,
    count,
    renewed,
    after,
    assembled,
    tile,
    top,
    vectors,
    factor,
    rows_ref,
    pvectors,
    pfactor,
    loaded,
    vt3,
    v3,
    tth,
    ttl,
    pt3,
    p3,
    st3,
    gv3,
    picks,
    ga,
    proj,
    uh,
    ul,
    upd,
    top_rx,
    z_tx,
    z_rx,
    chain_send,
    chain_recv,
    z_send,
    z_recv,
):
    front, row = lax.axis_index("front"), lax.axis_index("row")
    size, cols = tile.shape
    chunks = cols // CHUNK
    piece = size // PIECES
    spread, cap = rows_ref.shape
    slots = n_front * cap

    pairs = (
        (vectors_in, vectors),
        (tile_in, tile),
        (factor_in, factor),
        (top_in, top),
        (rows_in, rows_ref),
        (pvectors_in, pvectors),
        (pfactor_in, pfactor),
    )
    loads = [pltpu.make_async_copy(a, b, loaded.at[i]) for i, (a, b) in enumerate(pairs)]
    for load in loads:
        load.start()

    barrier = pltpu.get_barrier_semaphore()

    def greet(step, carry):
        peer = lax.rem(front + step, n_front)
        pl.semaphore_signal(barrier, inc=1, device_id={"front": peer}, device_id_type=MESH)
        return carry

    @pl.when(row > 0)
    def _():
        pl.semaphore_signal(barrier, inc=1, device_id={"row": row - 1}, device_id_type=MESH)

    lax.fori_loop(1, n_front, greet, 0)

    def columns(c):
        return pl.ds(pl.multiple_of(c * CHUNK, CHUNK), CHUNK)

    def project(c):
        proj[c] = dot(vt3[...], right_triple(tile[:, columns(c)]))

    def chain_copy(c, q):
        part = pl.ds(q * piece, piece)
        return pltpu.make_async_remote_copy(
            src_ref=after.at[part, columns(c)],
            dst_ref=top_rx.at[c, part],
            send_sem=chain_send.at[c, q],
            recv_sem=chain_recv.at[c, q],
            device_id={"row": lax.rem(row + 1, n_row)},
            device_id_type=MESH,
        )

    def chain(c):
        for q in range(PIECES):
            part = pl.ds(q * piece, piece)
            depth = min(size, -(-(q + 1) * piece // 128) * 128)

            @pl.when(row == 0)
            def _():
                top_rx[c, part] = top[part, columns(c)]

            @pl.when(row > 0)
            def _():
                chain_copy(c, q).wait_recv()

            entering = top_rx[c, part]
            high, low = split(entering + proj[c, part])
            uh[part], ul[part] = high, low
            update = (
                dot(tth[part, :depth], uh[:depth])
                + dot(tth[part, :depth], ul[:depth])
                + dot(ttl[part, :depth], uh[:depth])
            )
            after[part, columns(c)] = entering - update
            upd[part] = update

            @pl.when(row < n_row - 1)
            def _():
                chain_copy(c, q).start()

    def z_copy(c, target, source):
        return pltpu.make_async_remote_copy(
            src_ref=z_tx.at[c, target],
            dst_ref=z_rx.at[c, source],
            send_sem=z_send.at[c, target],
            recv_sem=z_recv.at[c, source],
            device_id={"front": target},
            device_id_type=MESH,
        )

    def contribute(c):
        weights = right_triple(upd[...])
        z_tx[c] = (ga[c] - dot(gv3[...], weights)).reshape(n_front, cap, CHUNK)

        def send(step, carry):
            z_copy(c, lax.rem(front + step, n_front), front).start()
            return carry

        lax.fori_loop(1, n_front, send, 0)
        z_rx[c, front] = z_tx[c, front]
        renewed[:, columns(c)] = tile[:, columns(c)] - dot(v3[...], weights)

    loads[0].wait()
    vt3[...] = left_triple(vectors[...].T)
    loads[2].wait()
    high, low = split(factor[...].T)
    tth[...], ttl[...] = high, low
    uh[...] = jnp.zeros_like(uh)
    ul[...] = jnp.zeros_like(ul)
    loads[1].wait()
    project(0)
    loads[3].wait()

    pl.semaphore_wait(barrier, n_front - 1 + jnp.where(row < n_row - 1, 1, 0))

    @pl.when(row == 0)
    def _():
        chain(0)

    for load in loads[4:]:
        load.wait()

    first = lax.rem(parent[front], n_front)
    lane = lax.broadcasted_iota(jnp.int32, (1, cap), 1)
    listed = []
    for g in range(n_front):
        k = lax.rem(g + n_front - first, n_front)
        held = jnp.minimum(k, spread - 1)
        sent = jnp.where(k < spread, count[held], 0)
        listed.append(jnp.where(lane < sent, rows_ref[pl.ds(held, 1), :], -1))
    wanted = jnp.concatenate(listed, axis=1)
    chosen = lax.broadcasted_iota(jnp.int32, (size, slots), 0) == wanted
    picks[...] = jnp.where(chosen, 1.0, 0.0).T.astype(BF16)

    vh, vl = split(vectors[...])
    v3[...] = jnp.concatenate([vh, vh, vl], axis=1)
    gvh = dot(picks[...], vh).astype(BF16)
    gv3[...] = jnp.concatenate([gvh, gvh, dot(picks[...], vl).astype(BF16)], axis=1)

    def prepare(c, carry):
        th, tl = split(tile[:, columns(c)])
        ga[c] = dot(picks[...], th) + dot(picks[...], tl)

        @pl.when(c > 0)
        def _():
            project(c)

        return carry

    lax.fori_loop(0, chunks, prepare, 0)
    p3[...] = left_triple(pvectors[...])
    pt3[...] = left_triple(pvectors[...].T)
    st3[...] = left_triple(pfactor[...].T)

    def forward(c, carry):
        @pl.when(jnp.logical_or(row > 0, c > 0))
        def _():
            chain(c)

        contribute(c)
        return carry

    lax.fori_loop(0, chunks, forward, 0)

    def assemble(c, carry):
        def arrive(step, inner):
            z_copy(c, front, lax.rem(front + step, n_front)).wait_recv()
            return inner

        lax.fori_loop(1, n_front, arrive, 0)
        stacked = z_rx[c].reshape(slots, CHUNK)
        inner_sums = dot(pt3[...], right_triple(stacked))
        weights = dot(st3[...], right_triple(inner_sums))
        assembled[:, columns(c)] = stacked - dot(p3[...], right_triple(weights))
        return carry

    lax.fori_loop(0, chunks, assemble, 0)

    def finish(c, carry):
        def left(step, inner):
            z_copy(c, lax.rem(front + step, n_front), front).wait_send()
            return inner

        lax.fori_loop(1, n_front, left, 0)

        @pl.when(row < n_row - 1)
        def _():
            for q in range(PIECES):
                chain_copy(c, q).wait_send()

        return carry

    lax.fori_loop(0, chunks, finish, 0)


def solution(mesh):
    n_front, n_row = mesh.shape["front"], mesh.shape["row"]

    def shards(tile, top, vectors, factor, parent, rows, count, pvectors, pfactor):
        size, cols = tile.shape[1:]
        stacked = pvectors.shape[1]
        cap = rows.shape[3]
        chunks = cols // CHUNK
        vmem = pl.BlockSpec(memory_space=pltpu.VMEM)
        smem = pl.BlockSpec(memory_space=pltpu.SMEM)
        hbm = pl.BlockSpec(memory_space=pltpu.HBM)
        outs = pl.pallas_call(
            functools.partial(kernel, n_front, n_row),
            out_shape=(
                jax.ShapeDtypeStruct((size, cols), F32),
                jax.ShapeDtypeStruct((size, cols), F32),
                jax.ShapeDtypeStruct((stacked, cols), F32),
            ),
            in_specs=[hbm] * 7 + [smem] * 2,
            out_specs=(vmem, vmem, vmem),
            scratch_shapes=[
                pltpu.VMEM((size, cols), F32),
                pltpu.VMEM((size, cols), F32),
                pltpu.VMEM((size, size), F32),
                pltpu.VMEM((size, size), F32),
                pltpu.VMEM(rows.shape[2:], jnp.int32),
                pltpu.VMEM((stacked, size), F32),
                pltpu.VMEM((size, size), F32),
                pltpu.SemaphoreType.DMA((7,)),
                pltpu.VMEM((size, 3 * size), BF16),
                pltpu.VMEM((size, 3 * size), BF16),
                pltpu.VMEM((size, size), BF16),
                pltpu.VMEM((size, size), BF16),
                pltpu.VMEM((size, 3 * stacked), BF16),
                pltpu.VMEM((stacked, 3 * size), BF16),
                pltpu.VMEM((size, 3 * size), BF16),
                pltpu.VMEM((stacked, 3 * size), BF16),
                pltpu.VMEM((stacked, size), BF16),
                pltpu.VMEM((chunks, stacked, CHUNK), F32),
                pltpu.VMEM((chunks, size, CHUNK), F32),
                pltpu.VMEM((size, CHUNK), BF16),
                pltpu.VMEM((size, CHUNK), BF16),
                pltpu.VMEM((size, CHUNK), F32),
                pltpu.VMEM((chunks, size, CHUNK), F32),
                pltpu.VMEM((chunks, n_front, cap, CHUNK), F32),
                pltpu.VMEM((chunks, n_front, cap, CHUNK), F32),
                pltpu.SemaphoreType.DMA((chunks, PIECES)),
                pltpu.SemaphoreType.DMA((chunks, PIECES)),
                pltpu.SemaphoreType.DMA((chunks, n_front)),
                pltpu.SemaphoreType.DMA((chunks, n_front)),
            ],
            compiler_params=pltpu.CompilerParams(
                collective_id=0, has_side_effects=True, vmem_limit_bytes=60 * 1024 * 1024
            ),
        )(tile[0], top[0], vectors[0], factor[0], rows[0, 0], pvectors[0], pfactor[0], parent, count[0, 0])
        return tuple(out[None] for out in outs)

    placed = (
        P("front", "row", "col"),
        P("front", None, "col"),
        P("front", "row", None),
        P("front", "row", None),
        P(),
        P("front", "row", None, None),
        P("front", "row", None),
        P("front", "row", None),
        P("front", "row", None),
    )
    out = P("front", "row", "col")
    return jax.shard_map(
        shards, mesh=mesh, in_specs=placed, out_specs=(out, out, out), check_vma=False
    )
```

time: 173 us -> 73.1 us (0.42)
  the two profiles are of different devices: /device:TPU:77 before, /device:TPU:113 now
where the time goes in v1:
time: 73.1 us; the launch traced here: 72.4 us
  Pallas kernels  68 us (93%)
  local copies, waits for them, and re-layouts  3.76 us (5%)
    pallas_call x1, Pallas kernels, shards(): pl.pallas_call(functools.partial(kernel, n_front, n_row), out_shape=(jax....  68 us
    unnamed x7, local copies, waits for them, and re-layouts  3.76 us

profile of v1, /device:TPU:113, one launch (start us, length us, event | category | flops | bytes accessed | tf_op | source)
XLA Modules:
  0.0 72.4 jit_solution(1144331812889745874)
XLA Ops:
  0.6 68.0 %shard_map.112 = (f32[256,512]{1,0:T(8,128)}, f32[256,512]{1,0:T(8,128)}, f32[512,512]{1,0:T(8,128)}) custom-call(f32[256,512]{1,0:T(8,128)} %bitcast.14, f32[256,512]{1,0:T(8,128)} %bitcast.15, f32[256,256]{1,0:T(8,128)} %bitcast.17, f32[256,256]{1,0:T(8,128)} %bitcast.18, s32[8,32]{1,0:T(8,128)} %bitcast.20, f32[512,256]{1,0:T(8,128)} %bitcast.16, ...), custom_call_target="tpu_custom_call" | custom-call | tf_op jit(solution)/shard_map/pallas_call | solution.py:284
  68.6 0.0 copy-start.1
  68.7 0.0 copy-start
  68.7 2.0 %copy.15 = f32[1,256,512]{2,1,0:T(8,128)} copy(f32[1,256,512]{2,1,0:T(8,128)} %bitcast.13) | data formatting | bytes 1048576
  70.6 0.0 copy-done.1
  70.7 0.8 %copy.16 = f32[1,256,512]{2,1,0:T(8,128)} copy(f32[1,256,512]{2,1,0:T(8,128)S(1)} %bitcast.12) | data formatting | bytes 1048576
  71.4 0.0 copy-done
  71.4 1.0 %copy.17 = f32[1,512,512]{2,1,0:T(8,128)} copy(f32[1,512,512]{2,1,0:T(8,128)S(1)} %bitcast.11) | data formatting | bytes 2097152
Async XLA Ops:
  68.6 2.0 %copy-start.1 = (f32[256,512]{1,0:T(8,128)S(1)}, f32[256,512]{1,0:T(8,128)}, u32[]{:S(2)}) copy-start(f32[256,512]{1,0:T(8,128)} %get-tuple-element.7) | copy-start | bytes 1572868
  68.7 2.8 %copy-start = (f32[512,512]{1,0:T(8,128)S(1)}, f32[512,512]{1,0:T(8,128)}, u32[]{:S(2)}) copy-start(f32[512,512]{1,0:T(8,128)} %get-tuple-element.8) | copy-start | bytes 3145732

commit v2 on v1

v2 whole, which is shorter than its diff:
```python
import functools

import jax
import jax.numpy as jnp
from jax import lax
from jax.experimental import pallas as pl
from jax.experimental.pallas import tpu as pltpu
from jax.sharding import PartitionSpec as P

MESH = pl.DeviceIdType.MESH
F32, BF16 = jnp.float32, jnp.bfloat16
CHUNK = 128
PIECES = 8
WIDE = 256


def split(x):
    high = x.astype(BF16)
    return high, (x - high.astype(F32)).astype(BF16)


def dot(left, right):
    return jnp.dot(left, right, preferred_element_type=F32)


def by_rows(left, right):
    lh, ll = split(left)
    rh, rl = split(right)
    return lax.dot_general(
        jnp.concatenate([lh, lh, ll], axis=1),
        jnp.concatenate([rh, rl, rh], axis=1),
        (((1,), (1,)), ((), ())),
        preferred_element_type=F32,
    )


def left_triple(x):
    high, low = split(x)
    return jnp.concatenate([high, high, low], axis=1)


def right_triple(x):
    high, low = split(x)
    return jnp.concatenate([high, low, high], axis=0)


def kernel(
    n_front,
    n_row,
    tile_in,
    top_in,
    vectors_in,
    factor_in,
    rows_in,
    pvectors_in,
    pfactor_in,
    parent_in,
    count_in,
    renewed,
    after,
    assembled,
    tile,
    vectors,
    factor,
    rows_ref,
    pvectors,
    pfactor,
    parent,
    count,
    loaded,
    top_loaded,
    vt3,
    tth,
    ttl,
    vf3,
    gvf3,
    picks,
    ga,
    proj,
    u3,
    h3,
    top_rx,
    z_tx,
    z_rx,
    chain_send,
    chain_recv,
    z_send,
    z_recv,
):
    front, row = lax.axis_index("front"), lax.axis_index("row")
    size, cols = tile.shape
    chunks = cols // CHUNK
    piece = size // PIECES
    spread, cap = rows_ref.shape
    slots = n_front * cap

    def top_load(c):
        return pltpu.make_async_copy(
            top_in.at[:, pl.ds(c * CHUNK, CHUNK)], top_rx.at[c], top_loaded.at[c]
        )

    pairs = (
        (vectors_in, vectors),
        (tile_in, tile),
        (factor_in, factor),
        (rows_in, rows_ref),
        (parent_in, parent),
        (count_in, count),
        (pvectors_in, pvectors),
        (pfactor_in, pfactor),
    )
    loads = [pltpu.make_async_copy(a, b, loaded.at[i]) for i, (a, b) in enumerate(pairs)]
    for load in loads[:3]:
        load.start()

    @pl.when(row == 0)
    def _():
        for c in range(chunks):
            top_load(c).start()

    for load in loads[3:]:
        load.start()

    barrier = pltpu.get_barrier_semaphore()

    def greet(step, carry):
        peer = lax.rem(front + step, n_front)
        pl.semaphore_signal(barrier, inc=1, device_id={"front": peer}, device_id_type=MESH)
        return carry

    @pl.when(row > 0)
    def _():
        pl.semaphore_signal(barrier, inc=1, device_id={"row": row - 1}, device_id_type=MESH)

    lax.fori_loop(1, n_front, greet, 0)

    def columns(c):
        return pl.ds(pl.multiple_of(c * CHUNK, CHUNK), CHUNK)

    def chain_copy(c, q):
        part = pl.ds(q * piece, piece)
        return pltpu.make_async_remote_copy(
            src_ref=after.at[part, columns(c)],
            dst_ref=top_rx.at[c, part],
            send_sem=chain_send.at[c, q],
            recv_sem=chain_recv.at[c, q],
            device_id={"row": lax.rem(row + 1, n_row)},
            device_id_type=MESH,
        )

    def chain(c):
        for q in range(PIECES):
            part = pl.ds(q * piece, piece)
            depth = min(size, -(-(q + 1) * piece // 128) * 128)

            @pl.when(row > 0)
            def _():
                chain_copy(c, q).wait_recv()

            entering = top_rx[c, part]
            high, low = split(entering + proj[part, columns(c)])
            u3[part, columns(c)] = high
            u3[pl.ds(size + q * piece, piece), columns(c)] = low
            u3[pl.ds(2 * size + q * piece, piece), columns(c)] = high
            first = u3[:depth, columns(c)]
            update = (
                dot(tth[part, :depth], first)
                + dot(tth[part, :depth], u3[size : size + depth, columns(c)])
                + dot(ttl[part, :depth], first)
            )
            after[part, columns(c)] = entering - update

            @pl.when(row < n_row - 1)
            def _():
                chain_copy(c, q).start()

    def z_copy(c, target, source):
        return pltpu.make_async_remote_copy(
            src_ref=z_tx.at[c, target],
            dst_ref=z_rx.at[c, source],
            send_sem=z_send.at[c, target],
            recv_sem=z_recv.at[c, source],
            device_id={"front": target},
            device_id_type=MESH,
        )

    def contribute(c):
        outgoing = ga[:, columns(c)] - dot(gvf3[...], u3[:, columns(c)])
        z_tx[c] = outgoing.reshape(n_front, cap, CHUNK)

        def send(step, carry):
            z_copy(c, lax.rem(front + step, n_front), front).start()
            return carry

        lax.fori_loop(1, n_front, send, 0)
        z_rx[c, front] = z_tx[c, front]

    loads[0].wait()
    vt3[...] = left_triple(vectors[...].T)
    loads[2].wait()
    high, low = split(factor[...].T)
    tth[...], ttl[...] = high, low
    loads[1].wait()
    proj[...] = dot(vt3[...], right_triple(tile[...]))
    u3[...] = jnp.zeros_like(u3)

    pl.semaphore_wait(barrier, n_front - 1 + jnp.where(row < n_row - 1, 1, 0))

    @pl.when(row == 0)
    def _():
        for c in range(chunks):
            top_load(c).wait()
        chain(0)

    for load in loads[3:]:
        load.wait()

    first = lax.rem(parent[front], n_front)
    lane = lax.broadcasted_iota(jnp.int32, (1, cap), 1)
    listed = []
    for g in range(n_front):
        k = lax.rem(g + n_front - first, n_front)
        held = jnp.minimum(k, spread - 1)
        sent = jnp.where(k < spread, count[held], 0)
        listed.append(jnp.where(lane < sent, rows_ref[pl.ds(held, 1), :], -1))
    wanted = jnp.concatenate(listed, axis=1)
    chosen = lax.broadcasted_iota(jnp.int32, (size, slots), 0) == wanted
    picks[...] = jnp.where(chosen, 1.0, 0.0).T.astype(BF16)

    vh, vl = split(by_rows(vectors[...], factor[...]))
    vf3[...] = jnp.concatenate([vh, vh, vl], axis=1)
    gvh = dot(picks[...], vh).astype(BF16)
    gvf3[...] = jnp.concatenate([gvh, gvh, dot(picks[...], vl).astype(BF16)], axis=1)
    th, tl = split(tile[...])
    ga[...] = dot(picks[...], th) + dot(picks[...], tl)

    def forward(c, carry):
        @pl.when(jnp.logical_or(row > 0, c > 0))
        def _():
            chain(c)

        contribute(c)
        return carry

    lax.fori_loop(0, chunks, forward, 0)

    renewed[...] = tile[...] - dot(vf3[...], u3[...])
    h3[...] = left_triple(by_rows(by_rows(pvectors[...], pfactor[...]), pvectors[...]))

    for w in range(cols // WIDE):
        mine = range(w * WIDE // CHUNK, (w + 1) * WIDE // CHUNK)

        def arrive(step, inner):
            for c in mine:
                z_copy(c, front, lax.rem(front + step, n_front)).wait_recv()
            return inner

        lax.fori_loop(1, n_front, arrive, 0)
        stacked = jnp.concatenate([z_rx[c].reshape(slots, CHUNK) for c in mine], axis=1)
        assembled[:, w * WIDE : (w + 1) * WIDE] = stacked - dot(h3[...], right_triple(stacked))

    def finish(c, carry):
        def left(step, inner):
            z_copy(c, lax.rem(front + step, n_front), front).wait_send()
            return inner

        lax.fori_loop(1, n_front, left, 0)

        @pl.when(row < n_row - 1)
        def _():
            for q in range(PIECES):
                chain_copy(c, q).wait_send()

        return carry

    lax.fori_loop(0, chunks, finish, 0)


def write_out(*refs):
    results, arrays, sems = refs[:3], refs[3:6], refs[6]
    copies = [
        pltpu.make_async_copy(result, array, sems.at[i])
        for i, (result, array) in enumerate(zip(results, arrays))
    ]
    for copy in copies:
        copy.start()
    for copy in copies:
        copy.wait()


def solution(mesh):
    n_front, n_row = mesh.shape["front"], mesh.shape["row"]

    def shards(tile, top, vectors, factor, parent, rows, count, pvectors, pfactor):
        size, cols = tile.shape[1:]
        stacked = pvectors.shape[1]
        cap = rows.shape[3]
        chunks = cols // CHUNK
        vmem = pl.BlockSpec(memory_space=pltpu.VMEM)
        hbm = pl.BlockSpec(memory_space=pltpu.HBM)
        shapes = (
            jax.ShapeDtypeStruct((size, cols), F32),
            jax.ShapeDtypeStruct((size, cols), F32),
            jax.ShapeDtypeStruct((stacked, cols), F32),
        )
        operands = (
            tile[0], top[0], vectors[0], factor[0], rows[0, 0], pvectors[0], pfactor[0], parent, count[0, 0],
        )
        outs = pl.pallas_call(
            functools.partial(kernel, n_front, n_row),
            out_shape=shapes,
            in_specs=[hbm] * 9,
            out_specs=(vmem, vmem, vmem),
            scratch_shapes=[
                pltpu.VMEM((size, cols), F32),
                pltpu.VMEM((size, size), F32),
                pltpu.VMEM((size, size), F32),
                pltpu.VMEM(rows.shape[2:], jnp.int32),
                pltpu.VMEM((stacked, size), F32),
                pltpu.VMEM((size, size), F32),
                pltpu.SMEM(parent.shape, jnp.int32),
                pltpu.SMEM(count.shape[2:], jnp.int32),
                pltpu.SemaphoreType.DMA((8,)),
                pltpu.SemaphoreType.DMA((chunks,)),
                pltpu.VMEM((size, 3 * size), BF16),
                pltpu.VMEM((size, size), BF16),
                pltpu.VMEM((size, size), BF16),
                pltpu.VMEM((size, 3 * size), BF16),
                pltpu.VMEM((stacked, 3 * size), BF16),
                pltpu.VMEM((stacked, size), BF16),
                pltpu.VMEM((stacked, cols), F32),
                pltpu.VMEM((size, cols), F32),
                pltpu.VMEM((3 * size, cols), BF16),
                pltpu.VMEM((stacked, 3 * stacked), BF16),
                pltpu.VMEM((chunks, size, CHUNK), F32),
                pltpu.VMEM((chunks, n_front, cap, CHUNK), F32),
                pltpu.VMEM((chunks, n_front, cap, CHUNK), F32),
                pltpu.SemaphoreType.DMA((chunks, PIECES)),
                pltpu.SemaphoreType.DMA((chunks, PIECES)),
                pltpu.SemaphoreType.DMA((chunks, n_front)),
                pltpu.SemaphoreType.DMA((chunks, n_front)),
            ],
            compiler_params=pltpu.CompilerParams(
                collective_id=0, has_side_effects=True, vmem_limit_bytes=40 * 1024 * 1024
            ),
        )(*[pltpu.with_memory_space_constraint(operand, pltpu.HBM) for operand in operands])
        outs = pl.pallas_call(
            write_out,
            out_shape=shapes,
            in_specs=[vmem] * 3,
            out_specs=(hbm, hbm, hbm),
            scratch_shapes=[pltpu.SemaphoreType.DMA((3,))],
        )(*[pltpu.with_memory_space_constraint(o, pltpu.VMEM) for o in outs])
        return tuple(out[None] for out in outs)

    placed = (
        P("front", "row", "col"),
        P("front", None, "col"),
        P("front", "row", None),
        P("front", "row", None),
        P(),
        P("front", "row", None, None),
        P("front", "row", None),
        P("front", "row", None),
        P("front", "row", None),
    )
    out = P("front", "row", "col")
    return jax.shard_map(
        shards, mesh=mesh, in_specs=placed, out_specs=(out, out, out), check_vma=False
    )
```

time: 73.1 us -> 66.2 us (0.906)
  local copies, waits for them, and re-layouts: 3.76 us -> 0 us
  Pallas kernels: 68 us -> 65.1 us
    unnamed x7 -> x0, local copies, waits for them, and re-layouts: 3.76 us -> none
    pallas_call x1 -> x2, Pallas kernels: 68 us -> 65.1 us  [the longest x1 63.7 us: shards(): pl.pallas_call(functools.partial(kernel, n_front, n_row), out_shape=shape...]
where the time goes in v2:
time: 66.2 us; the launch traced here: 65.7 us
  Pallas kernels  65.1 us (98%)
    pallas_call x1, Pallas kernels, shards(): pl.pallas_call(functools.partial(kernel, n_front, n_row), out_shape=shape...  63.7 us
    pallas_call x1, Pallas kernels, shards(): pl.pallas_call(write_out, out_shape=shapes, in_specs=[vmem] * 3, out_spec...  1.34 us

profile of v2, /device:TPU:113, one launch (start us, length us, event | category | flops | bytes accessed | tf_op | source)
XLA Modules:
  0.0 65.7 jit_solution(1017989973387400291)
XLA Ops:
  0.6 63.7 %shard_map.112 = (f32[256,512]{1,0:T(8,128)S(1)}, f32[256,512]{1,0:T(8,128)S(1)}, f32[512,512]{1,0:T(8,128)S(1)}) custom-call(f32[256,512]{1,0:T(8,128)} %bitcast.11, f32[256,512]{1,0:T(8,128)} %bitcast.12, f32[256,256]{1,0:T(8,128)} %bitcast.14, f32[256,256]{1,0:T(8,128)} %bitcast.15, s32[8,32]{1,0:T(8,128)} %bitcast.17, f32[512,256]{1,0:T(8,128)} %bitcast.13, ...), custom_call_target="tpu_custom_call" | custom-call | tf_op jit(solution)/shard_map/pallas_call | solution.py:309
  64.4 1.3 %shard_map.113 = (f32[256,512]{1,0:T(8,128)}, f32[256,512]{1,0:T(8,128)}, f32[512,512]{1,0:T(8,128)}) custom-call(f32[256,512]{1,0:T(8,128)S(1)} %get-tuple-element.9.refs_0_, f32[256,512]{1,0:T(8,128)S(1)} %get-tuple-element.10.refs_1_, f32[512,512]{1,0:T(8,128)S(1)} %get-tuple-element.11.refs_2_), custom_call_target="tpu_custom_call" | custom-call | tf_op jit(solution)/shard_map/pallas_call | solution.py:347

commit v3 on v2

--- a/solution.py
+++ b/solution.py
@@ -12,6 +12,7 @@
 CHUNK = 128
 PIECES = 8
 WIDE = 256
+EARLY = 4
 
 
 def split(x):
@@ -86,6 +87,8 @@
     chain_recv,
     z_send,
     z_recv,
+    fronts,
+    everyone,
 ):
     front, row = lax.axis_index("front"), lax.axis_index("row")
     size, cols = tile.shape
@@ -122,17 +125,29 @@
         load.start()
 
     barrier = pltpu.get_barrier_semaphore()
-
-    def greet(step, carry):
-        peer = lax.rem(front + step, n_front)
-        pl.semaphore_signal(barrier, inc=1, device_id={"front": peer}, device_id_type=MESH)
-        return carry
+    last = n_row - 1
+
+    def tell(sem, **device):
+        pl.semaphore_signal(sem, inc=1, device_id=device, device_id_type=MESH)
+
+    def tell_fronts(sem):
+        def one(step, carry):
+            tell(sem, front=lax.rem(front + step, n_front))
+            return carry
+
+        lax.fori_loop(1, n_front, one, 0)
 
     @pl.when(row > 0)
     def _():
-        pl.semaphore_signal(barrier, inc=1, device_id={"row": row - 1}, device_id_type=MESH)
-
-    lax.fori_loop(1, n_front, greet, 0)
+        tell(barrier, row=row - 1)
+
+    @pl.when(row < last)
+    def _():
+        tell(barrier, row=last)
+
+    @pl.when(row == last)
+    def _():
+        tell_fronts(barrier)
 
     def columns(c):
         return pl.ds(pl.multiple_of(c * CHUNK, CHUNK), CHUNK)
@@ -204,7 +219,9 @@
     proj[...] = dot(vt3[...], right_triple(tile[...]))
     u3[...] = jnp.zeros_like(u3)
 
-    pl.semaphore_wait(barrier, n_front - 1 + jnp.where(row < n_row - 1, 1, 0))
+    @pl.when(row < last)
+    def _():
+        pl.semaphore_wait(barrier, 1)
 
     @pl.when(row == 0)
     def _():
@@ -234,15 +251,46 @@
     th, tl = split(tile[...])
     ga[...] = dot(picks[...], th) + dot(picks[...], tl)
 
-    def forward(c, carry):
+    @pl.when(row == last)
+    def _():
+        pl.semaphore_wait(barrier, n_front - 1 + last)
+        tell_fronts(fronts)
+        pl.semaphore_wait(fronts, n_front - 1)
+        for r in range(last):
+            tell(everyone, row=r)
+
+    def walk(c):
         @pl.when(jnp.logical_or(row > 0, c > 0))
         def _():
             chain(c)
 
-        contribute(c)
-        return carry
-
-    lax.fori_loop(0, chunks, forward, 0)
+    @pl.when(row < EARLY)
+    def _():
+        def walk_on(c, carry):
+            walk(c)
+            return carry
+
+        def give(c, carry):
+            contribute(c)
+            return carry
+
+        lax.fori_loop(0, chunks, walk_on, 0)
+        pl.semaphore_wait(everyone, 1)
+        lax.fori_loop(0, chunks, give, 0)
+
+    @pl.when(row >= EARLY)
+    def _():
+        def both(c, carry):
+            walk(c)
+
+            @pl.when(jnp.logical_and(row < last, c == 0))
+            def _():
+                pl.semaphore_wait(everyone, 1)
+
+            contribute(c)
+            return carry
+
+        lax.fori_loop(0, chunks, both, 0)
 
     renewed[...] = tile[...] - dot(vf3[...], u3[...])
     h3[...] = left_triple(by_rows(by_rows(pvectors[...], pfactor[...]), pvectors[...]))
@@ -339,7 +387,8 @@
                 pltpu.SemaphoreType.DMA((chunks, PIECES)),
                 pltpu.SemaphoreType.DMA((chunks, n_front)),
                 pltpu.SemaphoreType.DMA((chunks, n_front)),
-            ],
+            ]
+            + [pltpu.SemaphoreType.REGULAR] * 2,
             compiler_params=pltpu.CompilerParams(
                 collective_id=0, has_side_effects=True, vmem_limit_bytes=40 * 1024 * 1024
             ),

time: 66.2 us -> 63.5 us (0.959)
  Pallas kernels: 65.1 us -> 62.6 us
    pallas_call x1, Pallas kernels: 63.7 us -> 61.2 us  [shards(): pl.pallas_call(functools.partial(kernel, n_front, n_row), out_shape=shape...]
where the time goes in v3:
time: 63.5 us; the launch traced here: 63.2 us
  Pallas kernels  62.6 us (99%)
  between operations  0.64 us (1%)
    pallas_call x1, Pallas kernels, shards(): pl.pallas_call(functools.partial(kernel, n_front, n_row), out_shape=shape...  61.2 us
    pallas_call x1, Pallas kernels, shards(): pl.pallas_call(write_out, out_shape=shapes, in_specs=[vmem] * 3, out_spec...  1.34 us

profile of v3, /device:TPU:113, one launch (start us, length us, event | category | flops | bytes accessed | tf_op | source)
XLA Modules:
  0.0 63.2 jit_solution(6232450036267495182)
XLA Ops:
  0.6 61.2 %shard_map.112 = (f32[256,512]{1,0:T(8,128)S(1)}, f32[256,512]{1,0:T(8,128)S(1)}, f32[512,512]{1,0:T(8,128)S(1)}) custom-call(f32[256,512]{1,0:T(8,128)} %bitcast.11, f32[256,512]{1,0:T(8,128)} %bitcast.12, f32[256,256]{1,0:T(8,128)} %bitcast.14, f32[256,256]{1,0:T(8,128)} %bitcast.15, s32[8,32]{1,0:T(8,128)} %bitcast.17, f32[512,256]{1,0:T(8,128)} %bitcast.13, ...), custom_call_target="tpu_custom_call" | custom-call | tf_op jit(solution)/shard_map/pallas_call | solution.py:357
  61.9 1.3 %shard_map.113 = (f32[256,512]{1,0:T(8,128)}, f32[256,512]{1,0:T(8,128)}, f32[512,512]{1,0:T(8,128)}) custom-call(f32[256,512]{1,0:T(8,128)S(1)} %get-tuple-element.9.refs_0_, f32[256,512]{1,0:T(8,128)S(1)} %get-tuple-element.10.refs_1_, f32[512,512]{1,0:T(8,128)S(1)} %get-tuple-element.11.refs_2_), custom_call_target="tpu_custom_call" | custom-call | tf_op jit(solution)/shard_map/pallas_call | solution.py:396

commit v4 on v3

--- a/solution.py
+++ b/solution.py
@@ -9,10 +9,9 @@
 
 MESH = pl.DeviceIdType.MESH
 F32, BF16 = jnp.float32, jnp.bfloat16
-CHUNK = 128
-PIECES = 8
-WIDE = 256
-EARLY = 4
+GROUPS = ((0, 128, 8), (128, 128, 8), (256, 128, 8), (384, 128, 8))
+PARTS = ((0, 128, 0), (128, 128, 1), (256, 256, 3))
+EARLY = 3
 
 
 def split(x):
@@ -92,15 +91,18 @@
 ):
     front, row = lax.axis_index("front"), lax.axis_index("row")
     size, cols = tile.shape
-    chunks = cols // CHUNK
-    piece = size // PIECES
+    groups = range(len(GROUPS))
     spread, cap = rows_ref.shape
     slots = n_front * cap
 
+    def columns(c):
+        return pl.ds(GROUPS[c][0], GROUPS[c][1])
+
+    def part_columns(c):
+        return pl.ds(PARTS[c][0], PARTS[c][1])
+
     def top_load(c):
-        return pltpu.make_async_copy(
-            top_in.at[:, pl.ds(c * CHUNK, CHUNK)], top_rx.at[c], top_loaded.at[c]
-        )
+        return pltpu.make_async_copy(top_in.at[:, columns(c)], top_rx.at[:, columns(c)], top_loaded.at[c])
 
     pairs = (
         (vectors_in, vectors),
@@ -118,7 +120,7 @@
 
     @pl.when(row == 0)
     def _():
-        for c in range(chunks):
+        for c in groups:
             top_load(c).start()
 
     for load in loads[3:]:
@@ -149,14 +151,12 @@
     def _():
         tell_fronts(barrier)
 
-    def columns(c):
-        return pl.ds(pl.multiple_of(c * CHUNK, CHUNK), CHUNK)
-
     def chain_copy(c, q):
+        piece = size // GROUPS[c][2]
         part = pl.ds(q * piece, piece)
         return pltpu.make_async_remote_copy(
             src_ref=after.at[part, columns(c)],
-            dst_ref=top_rx.at[c, part],
+            dst_ref=top_rx.at[part, columns(c)],
             send_sem=chain_send.at[c, q],
             recv_sem=chain_recv.at[c, q],
             device_id={"row": lax.rem(row + 1, n_row)},
@@ -164,7 +164,8 @@
         )
 
     def chain(c):
-        for q in range(PIECES):
+        piece = size // GROUPS[c][2]
+        for q in range(GROUPS[c][2]):
             part = pl.ds(q * piece, piece)
             depth = min(size, -(-(q + 1) * piece // 128) * 128)
 
@@ -172,7 +173,7 @@
             def _():
                 chain_copy(c, q).wait_recv()
 
-            entering = top_rx[c, part]
+            entering = top_rx[part, columns(c)]
             high, low = split(entering + proj[part, columns(c)])
             u3[part, columns(c)] = high
             u3[pl.ds(size + q * piece, piece), columns(c)] = low
@@ -191,8 +192,8 @@
 
     def z_copy(c, target, source):
         return pltpu.make_async_remote_copy(
-            src_ref=z_tx.at[c, target],
-            dst_ref=z_rx.at[c, source],
+            src_ref=z_tx.at[target, :, part_columns(c)],
+            dst_ref=z_rx.at[source, :, part_columns(c)],
             send_sem=z_send.at[c, target],
             recv_sem=z_recv.at[c, source],
             device_id={"front": target},
@@ -200,15 +201,24 @@
         )
 
     def contribute(c):
-        outgoing = ga[:, columns(c)] - dot(gvf3[...], u3[:, columns(c)])
-        z_tx[c] = outgoing.reshape(n_front, cap, CHUNK)
+        mine = part_columns(c)
+        outgoing = ga[:, mine] - dot(gvf3[...], u3[:, mine])
+        z_tx[:, :, mine] = outgoing.reshape(n_front, cap, PARTS[c][1])
 
         def send(step, carry):
             z_copy(c, lax.rem(front + step, n_front), front).start()
             return carry
 
         lax.fori_loop(1, n_front, send, 0)
-        z_rx[c, front] = z_tx[c, front]
+        z_rx[front, :, mine] = z_tx[front, :, mine]
+
+    @pl.when(row == last)
+    def _():
+        pl.semaphore_wait(barrier, n_front - 1 + last)
+        tell_fronts(fronts)
+        pl.semaphore_wait(fronts, n_front - 1)
+        for r in range(last):
+            tell(everyone, row=r)
 
     loads[0].wait()
     vt3[...] = left_triple(vectors[...].T)
@@ -216,8 +226,12 @@
     high, low = split(factor[...].T)
     tth[...], ttl[...] = high, low
     loads[1].wait()
-    proj[...] = dot(vt3[...], right_triple(tile[...]))
-    u3[...] = jnp.zeros_like(u3)
+
+    def project(mine):
+        proj[:, mine] = dot(vt3[...], right_triple(tile[:, mine]))
+        u3[:, mine] = jnp.zeros((3 * size, mine.size), BF16)
+
+    project(columns(0))
 
     @pl.when(row < last)
     def _():
@@ -225,10 +239,11 @@
 
     @pl.when(row == 0)
     def _():
-        for c in range(chunks):
+        for c in groups:
             top_load(c).wait()
         chain(0)
 
+    project(pl.ds(GROUPS[0][1], cols - GROUPS[0][1]))
     for load in loads[3:]:
         load.wait()
 
@@ -251,77 +266,56 @@
     th, tl = split(tile[...])
     ga[...] = dot(picks[...], th) + dot(picks[...], tl)
 
-    @pl.when(row == last)
-    def _():
-        pl.semaphore_wait(barrier, n_front - 1 + last)
-        tell_fronts(fronts)
-        pl.semaphore_wait(fronts, n_front - 1)
-        for r in range(last):
-            tell(everyone, row=r)
-
-    def walk(c):
-        @pl.when(jnp.logical_or(row > 0, c > 0))
-        def _():
-            chain(c)
-
-    @pl.when(row < EARLY)
-    def _():
-        def walk_on(c, carry):
-            walk(c)
-            return carry
-
-        def give(c, carry):
-            contribute(c)
-            return carry
-
-        lax.fori_loop(0, chunks, walk_on, 0)
-        pl.semaphore_wait(everyone, 1)
-        lax.fori_loop(0, chunks, give, 0)
-
-    @pl.when(row >= EARLY)
-    def _():
-        def both(c, carry):
-            walk(c)
-
-            @pl.when(jnp.logical_and(row < last, c == 0))
+    for c in groups:
+        if c == 0:
+
+            @pl.when(row > 0)
+            def _():
+                chain(c)
+
+            @pl.when(jnp.logical_and(row >= EARLY, row < last))
             def _():
                 pl.semaphore_wait(everyone, 1)
 
-            contribute(c)
-            return carry
-
-        lax.fori_loop(0, chunks, both, 0)
+        else:
+            chain(c)
+
+        for i, (_, _, needed) in enumerate(PARTS):
+            if needed == c:
+
+                @pl.when(row >= EARLY)
+                def _():
+                    contribute(i)
+
+    @pl.when(row < EARLY)
+    def _():
+        pl.semaphore_wait(everyone, 1)
+        for i in range(len(PARTS)):
+            contribute(i)
 
     renewed[...] = tile[...] - dot(vf3[...], u3[...])
     h3[...] = left_triple(by_rows(by_rows(pvectors[...], pfactor[...]), pvectors[...]))
 
-    for w in range(cols // WIDE):
-        mine = range(w * WIDE // CHUNK, (w + 1) * WIDE // CHUNK)
+    @pl.when(row < last)
+    def _():
+        for c in groups:
+            for q in range(GROUPS[c][2]):
+                chain_copy(c, q).wait_send()
+
+    for i, (start, width, _) in enumerate(PARTS):
+
+        def left(step, inner):
+            z_copy(i, lax.rem(front + step, n_front), front).wait_send()
+            return inner
 
         def arrive(step, inner):
-            for c in mine:
-                z_copy(c, front, lax.rem(front + step, n_front)).wait_recv()
+            z_copy(i, front, lax.rem(front + step, n_front)).wait_recv()
             return inner
 
+        lax.fori_loop(1, n_front, left, 0)
         lax.fori_loop(1, n_front, arrive, 0)
-        stacked = jnp.concatenate([z_rx[c].reshape(slots, CHUNK) for c in mine], axis=1)
-        assembled[:, w * WIDE : (w + 1) * WIDE] = stacked - dot(h3[...], right_triple(stacked))
-
-    def finish(c, carry):
-        def left(step, inner):
-            z_copy(c, lax.rem(front + step, n_front), front).wait_send()
-            return inner
-
-        lax.fori_loop(1, n_front, left, 0)
-
-        @pl.when(row < n_row - 1)
-        def _():
-            for q in range(PIECES):
-                chain_copy(c, q).wait_send()
-
-        return carry
-
-    lax.fori_loop(0, chunks, finish, 0)
+        stacked = z_rx[:, :, start : start + width].reshape(slots, width)
+        assembled[:, start : start + width] = stacked - dot(h3[...], right_triple(stacked))
 
 
 def write_out(*refs):
@@ -343,7 +337,8 @@
         size, cols = tile.shape[1:]
         stacked = pvectors.shape[1]
         cap = rows.shape[3]
-        chunks = cols // CHUNK
+        groups = len(GROUPS)
+        pieces = max(pieces for _, _, pieces in GROUPS)
         vmem = pl.BlockSpec(memory_space=pltpu.VMEM)
         hbm = pl.BlockSpec(memory_space=pltpu.HBM)
         shapes = (
@@ -369,7 +364,7 @@
                 pltpu.SMEM(parent.shape, jnp.int32),
                 pltpu.SMEM(count.shape[2:], jnp.int32),
                 pltpu.SemaphoreType.DMA((8,)),
-                pltpu.SemaphoreType.DMA((chunks,)),
+                pltpu.SemaphoreType.DMA((groups,)),
                 pltpu.VMEM((size, 3 * size), BF16),
                 pltpu.VMEM((size, size), BF16),
                 pltpu.VMEM((size, size), BF16),
@@ -380,13 +375,13 @@
                 pltpu.VMEM((size, cols), F32),
                 pltpu.VMEM((3 * size, cols), BF16),
                 pltpu.VMEM((stacked, 3 * stacked), BF16),
-                pltpu.VMEM((chunks, size, CHUNK), F32),
-                pltpu.VMEM((chunks, n_front, cap, CHUNK), F32),
-                pltpu.VMEM((chunks, n_front, cap, CHUNK), F32),
-                pltpu.SemaphoreType.DMA((chunks, PIECES)),
-                pltpu.SemaphoreType.DMA((chunks, PIECES)),
-                pltpu.SemaphoreType.DMA((chunks, n_front)),
-                pltpu.SemaphoreType.DMA((chunks, n_front)),
+                pltpu.VMEM((size, cols), F32),
+                pltpu.VMEM((n_front, cap, cols), F32),
+                pltpu.VMEM((n_front, cap, cols), F32),
+                pltpu.SemaphoreType.DMA((groups, pieces)),
+                pltpu.SemaphoreType.DMA((groups, pieces)),
+                pltpu.SemaphoreType.DMA((len(PARTS), n_front)),
+                pltpu.SemaphoreType.DMA((len(PARTS), n_front)),
             ]
             + [pltpu.SemaphoreType.REGULAR] * 2,
             compiler_params=pltpu.CompilerParams(

time: 63.5 us -> 62.6 us (0.986)
  Pallas kernels: 62.6 us -> 61.8 us
    pallas_call x1, Pallas kernels: 61.2 us -> 60.4 us  [shards(): pl.pallas_call(functools.partial(kernel, n_front, n_row), out_shape=shape...]
where the time goes in v4:
time: 62.6 us; the launch traced here: 62.4 us
  Pallas kernels  61.8 us (99%)
  between operations  0.64 us (1%)
    pallas_call x1, Pallas kernels, shards(): pl.pallas_call(functools.partial(kernel, n_front, n_row), out_shape=shape...  60.4 us
    pallas_call x1, Pallas kernels, shards(): pl.pallas_call(write_out, out_shape=shapes, in_specs=[vmem] * 3, out_spec...  1.34 us

profile of v4, /device:TPU:113, one launch (start us, length us, event | category | flops | bytes accessed | tf_op | source)
XLA Modules:
  0.0 62.4 jit_solution(17382945429701970827)
XLA Ops:
  0.6 60.4 %shard_map.112 = (f32[256,512]{1,0:T(8,128)S(1)}, f32[256,512]{1,0:T(8,128)S(1)}, f32[512,512]{1,0:T(8,128)S(1)}) custom-call(f32[256,512]{1,0:T(8,128)} %bitcast.11, f32[256,512]{1,0:T(8,128)} %bitcast.12, f32[256,256]{1,0:T(8,128)} %bitcast.14, f32[256,256]{1,0:T(8,128)} %bitcast.15, s32[8,32]{1,0:T(8,128)} %bitcast.17, f32[512,256]{1,0:T(8,128)} %bitcast.13, ...), custom_call_target="tpu_custom_call" | custom-call | tf_op jit(solution)/shard_map/pallas_call | solution.py:352
  61.1 1.3 %shard_map.113 = (f32[256,512]{1,0:T(8,128)}, f32[256,512]{1,0:T(8,128)}, f32[512,512]{1,0:T(8,128)}) custom-call(f32[256,512]{1,0:T(8,128)S(1)} %get-tuple-element.9.refs_0_, f32[256,512]{1,0:T(8,128)S(1)} %get-tuple-element.10.refs_1_, f32[512,512]{1,0:T(8,128)S(1)} %get-tuple-element.11.refs_2_), custom_call_target="tpu_custom_call" | custom-call | tf_op jit(solution)/shard_map/pallas_call | solution.py:391

commit v5 on v4

--- a/solution.py
+++ b/solution.py
@@ -11,7 +11,7 @@
 F32, BF16 = jnp.float32, jnp.bfloat16
 GROUPS = ((0, 128, 8), (128, 128, 8), (256, 128, 8), (384, 128, 8))
 PARTS = ((0, 128, 0), (128, 128, 1), (256, 256, 3))
-EARLY = 3
+EARLY = 5
 
 
 def split(x):
@@ -205,11 +205,17 @@
         outgoing = ga[:, mine] - dot(gvf3[...], u3[:, mine])
         z_tx[:, :, mine] = outgoing.reshape(n_front, cap, PARTS[c][1])
 
-        def send(step, carry):
-            z_copy(c, lax.rem(front + step, n_front), front).start()
+        def across(step, carry):
+            z_copy(c, (1 - half) * (n_front // 2) + lax.rem(place + step, n_front // 2), front).start()
             return carry
 
-        lax.fori_loop(1, n_front, send, 0)
+        def along(step, carry):
+            z_copy(c, half * (n_front // 2) + lax.rem(place + step, n_front // 2), front).start()
+            return carry
+
+        half, place = lax.div(front, n_front // 2), lax.rem(front, n_front // 2)
+        lax.fori_loop(0, n_front // 2, across, 0)
+        lax.fori_loop(1, n_front // 2, along, 0)
         z_rx[front, :, mine] = z_tx[front, :, mine]
 
     @pl.when(row == last)

time: 62.6 us -> 60.5 us (0.966)
  Pallas kernels: 61.8 us -> 59.6 us
    pallas_call x1, Pallas kernels: 60.4 us -> 58.3 us  [shards(): pl.pallas_call(functools.partial(kernel, n_front, n_row), out_shape=shape...]
where the time goes in v5:
time: 60.5 us; the launch traced here: 60.2 us
  Pallas kernels  59.6 us (99%)
  between operations  0.64 us (1%)
    pallas_call x1, Pallas kernels, shards(): pl.pallas_call(functools.partial(kernel, n_front, n_row), out_shape=shape...  58.3 us
    pallas_call x1, Pallas kernels, shards(): pl.pallas_call(write_out, out_shape=shapes, in_specs=[vmem] * 3, out_spec...  1.34 us

profile of v5, /device:TPU:113, one launch (start us, length us, event | category | flops | bytes accessed | tf_op | source)
XLA Modules:
  0.0 60.2 jit_solution(9868756454857941392)
XLA Ops:
  0.6 58.3 %shard_map.112 = (f32[256,512]{1,0:T(8,128)S(1)}, f32[256,512]{1,0:T(8,128)S(1)}, f32[512,512]{1,0:T(8,128)S(1)}) custom-call(f32[256,512]{1,0:T(8,128)} %bitcast.11, f32[256,512]{1,0:T(8,128)} %bitcast.12, f32[256,256]{1,0:T(8,128)} %bitcast.14, f32[256,256]{1,0:T(8,128)} %bitcast.15, s32[8,32]{1,0:T(8,128)} %bitcast.17, f32[512,256]{1,0:T(8,128)} %bitcast.13, ...), custom_call_target="tpu_custom_call" | custom-call | tf_op jit(solution)/shard_map/pallas_call | solution.py:358
  58.9 1.3 %shard_map.113 = (f32[256,512]{1,0:T(8,128)}, f32[256,512]{1,0:T(8,128)}, f32[512,512]{1,0:T(8,128)}) custom-call(f32[256,512]{1,0:T(8,128)S(1)} %get-tuple-element.9.refs_0_, f32[256,512]{1,0:T(8,128)S(1)} %get-tuple-element.10.refs_1_, f32[512,512]{1,0:T(8,128)S(1)} %get-tuple-element.11.refs_2_), custom_call_target="tpu_custom_call" | custom-call | tf_op jit(solution)/shard_map/pallas_call | solution.py:397

commit v6 on v5

--- a/solution.py
+++ b/solution.py
@@ -11,7 +11,7 @@
 F32, BF16 = jnp.float32, jnp.bfloat16
 GROUPS = ((0, 128, 8), (128, 128, 8), (256, 128, 8), (384, 128, 8))
 PARTS = ((0, 128, 0), (128, 128, 1), (256, 256, 3))
-EARLY = 5
+LAGS = (6, 4, 3)
 
 
 def split(x):
@@ -247,7 +247,13 @@
     def _():
         for c in groups:
             top_load(c).wait()
-        chain(0)
+        mine = columns(0)
+        high, low = split(top_rx[:, mine] + proj[:, mine])
+        u3[:size, mine], u3[size : 2 * size, mine], u3[2 * size :, mine] = high, low, high
+        update = dot(tth[...], high) + dot(tth[...], low) + dot(ttl[...], high)
+        after[:, mine] = top_rx[:, mine] - update
+        for q in range(GROUPS[0][2]):
+            chain_copy(0, q).start()
 
     project(pl.ds(GROUPS[0][1], cols - GROUPS[0][1]))
     for load in loads[3:]:
@@ -272,6 +278,7 @@
     th, tl = split(tile[...])
     ga[...] = dot(picks[...], th) + dot(picks[...], tl)
 
+    lag = sum(jnp.where(row < bound, 1, 0) for bound in LAGS)
     for c in groups:
         if c == 0:
 
@@ -279,24 +286,30 @@
             def _():
                 chain(c)
 
-            @pl.when(jnp.logical_and(row >= EARLY, row < last))
+            @pl.when(jnp.logical_and(lag == 0, row < last))
             def _():
                 pl.semaphore_wait(everyone, 1)
 
         else:
             chain(c)
 
+        if 0 < c < len(LAGS) + 1:
+
+            @pl.when(lag == c)
+            def _():
+                pl.semaphore_wait(everyone, 1)
+
         for i, (_, _, needed) in enumerate(PARTS):
-            if needed == c:
-
-                @pl.when(row >= EARLY)
+            if c >= needed:
+
+                @pl.when(lag == c - needed)
                 def _():
                     contribute(i)
 
-    @pl.when(row < EARLY)
-    def _():
-        pl.semaphore_wait(everyone, 1)
-        for i in range(len(PARTS)):
+    for i, (_, _, needed) in enumerate(PARTS):
+
+        @pl.when(lag > len(GROUPS) - 1 - needed)
+        def _():
             contribute(i)
 
     renewed[...] = tile[...] - dot(vf3[...], u3[...])

time: 60.5 us -> 60.3 us (level)
  no operation moved by 1% of the time
where the time goes in v6:
time: 60.3 us; the launch traced here: 60 us
  Pallas kernels  59.4 us (99%)
  between operations  0.64 us (1%)
    pallas_call x1, Pallas kernels, shards(): pl.pallas_call(functools.partial(kernel, n_front, n_row), out_shape=shape...  58 us
    pallas_call x1, Pallas kernels, shards(): pl.pallas_call(write_out, out_shape=shapes, in_specs=[vmem] * 3, out_spec...  1.34 us

profile of v6, /device:TPU:113, one launch (start us, length us, event | category | flops | bytes accessed | tf_op | source)
XLA Modules:
  0.0 60.0 jit_solution(12366324815366057539)
XLA Ops:
  0.6 58.0 %shard_map.112 = (f32[256,512]{1,0:T(8,128)S(1)}, f32[256,512]{1,0:T(8,128)S(1)}, f32[512,512]{1,0:T(8,128)S(1)}) custom-call(f32[256,512]{1,0:T(8,128)} %bitcast.11, f32[256,512]{1,0:T(8,128)} %bitcast.12, f32[256,256]{1,0:T(8,128)} %bitcast.14, f32[256,256]{1,0:T(8,128)} %bitcast.15, s32[8,32]{1,0:T(8,128)} %bitcast.17, f32[512,256]{1,0:T(8,128)} %bitcast.13, ...), custom_call_target="tpu_custom_call" | custom-call | tf_op jit(solution)/shard_map/pallas_call | solution.py:371
  58.7 1.3 %shard_map.113 = (f32[256,512]{1,0:T(8,128)}, f32[256,512]{1,0:T(8,128)}, f32[512,512]{1,0:T(8,128)}) custom-call(f32[256,512]{1,0:T(8,128)S(1)} %get-tuple-element.9.refs_0_, f32[256,512]{1,0:T(8,128)S(1)} %get-tuple-element.10.refs_1_, f32[512,512]{1,0:T(8,128)S(1)} %get-tuple-element.11.refs_2_), custom_call_target="tpu_custom_call" | custom-call | tf_op jit(solution)/shard_map/pallas_call | solution.py:410
